TPU v7x, 32 devices: a whole 2x2x4 slice. The times are simulated.
32 devices in a mesh: dp: 4 (over z), mp: 8 (over y, x, core).
Axes of the slice: x: 2, y: 2, z: 4, core: 2. Of those that a mesh axis runs over, the one named last changes fastest.
Arguments:
- guess_vectors: bfloat16 [128, 16, 4096], P(('dp', 'mp')), may hold values from -6 to 6
- preceding_symbol_vector: bfloat16 [128, 4096], P(('dp', 'mp')), may hold values from -6 to 6
- earlier_memory_matrix: float32 [128, 64, 64, 64], P('dp', 'mp'), may hold values from -4 to 4
- lag_blend_factor: float32 [4096], replicated, may hold values from 0 to 1
- constant_lag_blends: float32 [5, 4096], replicated, may hold values from 0 to 1
- blending_lower_matrix: bfloat16 [4096, 160], replicated, may hold values from -0.09375 to 0.09375
- blending_raise_matrix: bfloat16 [5, 32, 4096], replicated, may hold values from -1 to 1
- constant_fading: float32 [4096], P('mp'), may hold values from -6 to -1
- fading_lower_matrix: bfloat16 [4096, 64], replicated, may hold values from -0.09375 to 0.09375
- fading_raise_matrix: bfloat16 [64, 4096], P(None, 'mp'), may hold values from -1 to 1
- diagonal_boost: float32 [64, 64], P('mp'), may hold values from -3 to 3
- acceptor_matrix: bfloat16 [4096, 4096], P('dp', 'mp'), may hold values from -0.09375 to 0.09375
- lookup_matrix: bfloat16 [4096, 4096], P('dp', 'mp'), may hold values from -0.09375 to 0.09375
- payload_matrix: bfloat16 [4096, 4096], P('dp', 'mp'), may hold values from -0.09375 to 0.09375
- gating_matrix: bfloat16 [4096, 4096], P('dp', 'mp'), may hold values from -0.09375 to 0.09375
- emission_matrix: bfloat16 [4096, 4096], P('mp', 'dp'), may hold values from -0.09375 to 0.09375
- groupwise_scaling_factor: float32 [4096], P('mp'), may hold values from 0.1 to 1.9
- groupwise_scaling_offset: float32 [4096], P('mp'), may hold values from -3 to 3
- usable_guess_amount: int32 [128], replicated, may hold values from 1 to 16, as said below
- approved_guesses: int32 [128], replicated, may hold values from 0 to 16, as said below
- destination_slot: int32 [128], replicated, may hold values from 0 to 127, as said below
Outputs:
- layer_out: bfloat16 [128, 16, 4096], P(('dp', 'mp'))
- next_state: float32 [128, 64, 64, 64], P('dp', 'mp')
- next_edge: bfloat16 [128, 4096], P('dp', 'mp')
Inputs may be any that keep to these rules, and one draw needn't show every extreme that they name: `usable_guess_amount`: some request has all 16 draft tokens valid. approved_guesses[b] <= usable_guess_amount[b]; some request accepts all 16. destination_slot is a permutation of the requests. Of the 32 requests of one aligned block, at most 16 have owner slots in one aligned block of 32 slots, and some pair of blocks reaches 16.
All inputs are finite; a program needn't handle non-finite values.
Results may differ from a plain program's by a relative error of at most 0.007.
Values may be sent and summed in bfloat16 or wider, within the bound.
A program may use at most 256 MiB of HBM per device.

v0:
```python
import jax
import jax.numpy as jnp
from jax import lax
from jax.sharding import PartitionSpec as P

GROUP_DIMENSION = 64
norm_eps = 0.00064


def token_mixes(
    guess_vectors,
    edges,
    lag_blend_factor,
    constant_lag_blends,
    blending_lower_matrix,
    blending_raise_matrix,
):
    previous = jnp.concatenate([edges[:, None, :], guess_vectors[:, :-1, :]], axis=1)
    width = guess_vectors.shape[-1]
    current_input = guess_vectors.reshape(-1, width).astype(jnp.float32)
    shift_difference = previous.reshape(-1, width).astype(jnp.float32) - current_input
    shift_blended = (current_input + shift_difference * lag_blend_factor).astype(jnp.bfloat16)
    mixing_inner_all = jnp.tanh(
        jnp.dot(shift_blended, blending_lower_matrix, preferred_element_type=jnp.float32)
    ).astype(jnp.bfloat16)
    mixing_inner_width = blending_raise_matrix.shape[1]
    shift_mixed_rows = []
    for mix_component in range(5):
        mixing_inner_part = jnp.dot(
            mixing_inner_all[
                :, mix_component * mixing_inner_width : (mix_component + 1) * mixing_inner_width
            ],
            blending_raise_matrix[mix_component],
            preferred_element_type=jnp.float32,
        )
        shift_mixed_rows.append(
            (
                current_input
                + shift_difference * (constant_lag_blends[mix_component] + mixing_inner_part)
            ).astype(jnp.bfloat16)
        )
    return shift_mixed_rows


def wkv_blocks(
    acceptor_vectors,
    lookup_vectors,
    payload_vectors,
    logarithmic_fading_entries,
    diagonal_boost,
    starting_memory,
    approved_guesses,
):
    draft = acceptor_vectors.shape[1]
    cumulative = jnp.cumsum(logarithmic_fading_entries, axis=1)
    starts = jnp.concatenate(
        [jnp.zeros_like(logarithmic_fading_entries[:, :1]), cumulative], axis=1
    )
    before = starts[:, :draft]
    from_start = jnp.einsum(
        "bthi,bhij->bthj",
        acceptor_vectors * jnp.exp(before),
        starting_memory,
        precision=lax.Precision.HIGHEST,
    )
    later = jnp.arange(draft)[:, None] > jnp.arange(draft)[None, :]
    exponent = before[:, :, None] - cumulative[:, None, :]
    exponent = jnp.where(later[None, :, :, None, None], exponent, -1e30)
    scores = jnp.sum(
        acceptor_vectors[:, :, None] * lookup_vectors[:, None, :] * jnp.exp(exponent), axis=-1
    )
    inner = jnp.einsum("btsh,bshj->bthj", scores, payload_vectors, precision=lax.Precision.HIGHEST)
    diagonal_boost_contribution = (
        jnp.sum(acceptor_vectors * diagonal_boost * lookup_vectors, axis=-1, keepdims=True)
        * payload_vectors
    )
    outputs = from_start + inner + diagonal_boost_contribution
    at_accept = jnp.take_along_axis(starts, approved_guesses[:, None, None, None], axis=1)[:, 0]
    used = jnp.arange(draft)[None, :] < approved_guesses[:, None]
    coef_exp = jnp.where(used[:, :, None, None], at_accept[:, None] - cumulative, -1e30)
    weighted = jnp.exp(coef_exp) * lookup_vectors
    picked = jnp.exp(at_accept)[..., None] * starting_memory + jnp.einsum(
        "bshi,bshj->bhij", weighted, payload_vectors, precision=lax.Precision.HIGHEST
    )
    return (outputs, picked)


def gated_norm(outputs, gate_raw, gain, bias):
    centre = jnp.mean(outputs, axis=-1, keepdims=True)
    spread = outputs - centre
    variance = jnp.mean(spread * spread, axis=-1, keepdims=True)
    normed = (spread * lax.rsqrt(variance + norm_eps)).reshape(outputs.shape[0], -1)
    return ((normed * gain + bias) * jax.nn.silu(gate_raw)).astype(jnp.bfloat16)


def on_device(
    guess_vectors,
    preceding_symbol_vector,
    earlier_memory_matrix,
    lag_blend_factor,
    constant_lag_blends,
    blending_lower_matrix,
    blending_raise_matrix,
    constant_fading,
    fading_lower_matrix,
    fading_raise_matrix,
    diagonal_boost,
    acceptor_matrix,
    lookup_matrix,
    payload_matrix,
    gating_matrix,
    emission_matrix,
    groupwise_scaling_factor,
    groupwise_scaling_offset,
    usable_guess_amount,
    approved_guesses,
    destination_slot,
):
    own_reqs, draft, width = guess_vectors.shape
    group_count = lax.axis_size("mp")
    row_groups = lax.axis_size("dp")
    row_reqs = own_reqs * group_count
    row_index = lax.axis_index("dp")
    group_index = lax.axis_index("mp")
    local_width = acceptor_matrix.shape[1]
    local_heads = local_width // GROUP_DIMENSION
    gathered, edges_all = (
        lax.all_gather(guess_vectors, "mp", axis=0, tiled=True),
        lax.all_gather(preceding_symbol_vector, "mp", axis=0, tiled=True),
    )
    shift_mixed_rows = token_mixes(
        gathered,
        edges_all,
        lag_blend_factor,
        constant_lag_blends,
        blending_lower_matrix,
        blending_raise_matrix,
    )
    token_rows = row_reqs * draft
    sources = (shift_mixed_rows[3], shift_mixed_rows[1], shift_mixed_rows[2], shift_mixed_rows[4])
    pieces = (
        lax.all_gather(acceptor_matrix, "dp", axis=0, tiled=True),
        lax.all_gather(lookup_matrix, "dp", axis=0, tiled=True),
        lax.all_gather(payload_matrix, "dp", axis=0, tiled=True),
        lax.all_gather(gating_matrix, "dp", axis=0, tiled=True),
    )
    acceptor_vectors, lookup_vectors, payload_vectors, gate_raw = tuple(
        (
            jnp.dot(source_rows, piece, preferred_element_type=jnp.float32)
            for source_rows, piece in zip(sources, pieces)
        )
    )
    decay_inner_rows = jnp.tanh(
        jnp.dot(shift_mixed_rows[0], fading_lower_matrix, preferred_element_type=jnp.float32)
    ).astype(jnp.bfloat16)
    logarithmic_fading_entries = -jnp.exp(
        constant_fading
        + jnp.dot(decay_inner_rows, fading_raise_matrix, preferred_element_type=jnp.float32)
    )

    def to_heads(values):
        return values.reshape(row_reqs, draft, local_heads, GROUP_DIMENSION)

    row_accepted = lax.dynamic_slice_in_dim(approved_guesses, row_index * row_reqs, row_reqs)
    outputs, picked = wkv_blocks(
        to_heads(acceptor_vectors),
        to_heads(lookup_vectors),
        to_heads(payload_vectors),
        to_heads(logarithmic_fading_entries),
        diagonal_boost,
        earlier_memory_matrix,
        row_accepted,
    )
    hidden = gated_norm(
        outputs.reshape(token_rows, local_heads, GROUP_DIMENSION),
        gate_raw,
        groupwise_scaling_factor,
        groupwise_scaling_offset,
    )
    out_cols = lax.all_gather(emission_matrix, "dp", axis=1, tiled=True)
    attended = lax.psum_scatter(
        jnp.dot(hidden, out_cols, preferred_element_type=jnp.float32).astype(jnp.bfloat16),
        "mp",
        scatter_dimension=0,
        tiled=True,
    ).astype(jnp.float32)
    own_start = (row_index * group_count + group_index) * own_reqs
    own_lengths = lax.dynamic_slice_in_dim(usable_guess_amount, own_start, own_reqs)
    valid_mask = jnp.arange(draft, dtype=jnp.int32)[None, :] < own_lengths[:, None]
    layer_out = (
        guess_vectors.astype(jnp.float32)
        + jnp.where(
            valid_mask[..., None],
            attended.reshape(own_reqs, draft, width),
            jnp.zeros((), jnp.float32),
        )
    ).astype(jnp.bfloat16)
    edge_rows = jnp.concatenate([edges_all[:, None, :], gathered], axis=1)
    edge_cols = lax.dynamic_slice_in_dim(edge_rows, group_index * local_width, local_width, 2)
    chosen = jnp.take_along_axis(edge_cols, row_accepted[:, None, None], axis=1)[:, 0]
    capacity = 2 * row_reqs // row_groups
    target_rows = (destination_slot // row_reqs).reshape(row_groups, row_reqs)
    onehot = (
        target_rows[:, :, None] == jnp.arange(row_groups, dtype=jnp.int32)[None, None, :]
    ).astype(jnp.int32)
    earlier = jnp.cumsum(onehot, axis=1) - onehot
    ranks = jnp.sum(earlier * onehot, axis=-1)
    my_targets = lax.dynamic_index_in_dim(target_rows, row_index, 0, keepdims=False)
    my_ranks = lax.dynamic_index_in_dim(ranks, row_index, 0, keepdims=False)
    selected = (
        my_targets[:, None, None] == jnp.arange(row_groups, dtype=jnp.int32)[None, :, None]
    ) & (my_ranks[:, None, None] == jnp.arange(capacity, dtype=jnp.int32)[None, None, :])
    source_index = jnp.sum(
        selected.astype(jnp.int32) * jnp.arange(row_reqs, dtype=jnp.int32)[:, None, None], axis=0
    )
    filled = jnp.any(selected, axis=0)
    send_state = jnp.where(
        filled[..., None, None, None], picked[source_index], jnp.zeros((), jnp.float32)
    )
    send_edge = jnp.where(
        filled[..., None], chosen[source_index].astype(jnp.float32), jnp.zeros((), jnp.float32)
    )
    recv_state, recv_edge = (
        lax.all_to_all(
            send_state.astype(jnp.bfloat16), "dp", split_axis=0, concat_axis=0, tiled=True
        ).astype(send_state.dtype),
        lax.all_to_all(
            send_edge.astype(jnp.bfloat16), "dp", split_axis=0, concat_axis=0, tiled=True
        ).astype(send_edge.dtype),
    )
    wanted = row_index * row_reqs + jnp.arange(row_reqs, dtype=jnp.int32)
    total_reqs = destination_slot.shape[0]
    matches = (destination_slot[None, :] == wanted[:, None]).astype(jnp.int32)
    which = jnp.sum(matches * jnp.arange(total_reqs, dtype=jnp.int32)[None, :], axis=1)
    flat_index = which // row_reqs * capacity + ranks.reshape(-1)[which]
    next_state = recv_state.reshape(
        row_groups * capacity, local_heads, GROUP_DIMENSION, GROUP_DIMENSION
    )[flat_index]
    next_edge = recv_edge.reshape(row_groups * capacity, local_width)[flat_index].astype(
        jnp.bfloat16
    )
    return (layer_out, next_state, next_edge)


def solution(mesh):
    in_specs = (
        P(("dp", "mp"), None, None),
        P(("dp", "mp"), None),
        P("dp", "mp", None, None),
        P(),
        P(),
        P(),
        P(),
        P("mp"),
        P(),
        P(None, "mp"),
        P("mp", None),
        P("dp", "mp"),
        P("dp", "mp"),
        P("dp", "mp"),
        P("dp", "mp"),
        P("mp", "dp"),
        P("mp"),
        P("mp"),
        P(),
        P(),
        P(),
    )
    out_specs = (P(("dp", "mp"), None, None), P("dp", "mp", None, None), P("dp", "mp"))
    return jax.shard_map(
        on_device, mesh=mesh, in_specs=in_specs, out_specs=out_specs, check_vma=False
    )
```

profile of v0, /device:TPU:0, one launch (start us, length us, event | category | flops | bytes accessed | tf_op | source)
XLA Modules:
  0.0 585.9 jit_solution(18396825524794450216)
XLA Ops:
  12.2 10.8 %all-gather = bf16[8,4,4096]{2,1,0:T(4,128)(2,1)S(1)} all-gather(bf16[1,4,4096]{2,1,0:T(4,128)(2,1)S(1)} %bitcast.122), channel_id=1, replica_groups=mesh['dp'=4,'mp'=8] {'mp'}, dimensions={0}, use_global_device_ids=true | all-gather | bytes 294912 | tf_op jit(solution)/shard_map/all_gather | solution.py:129
  23.9 25.6 %all-gather.8.cloned.1.call-done = bf16[32,16,4096]{2,1,0:T(8,128)(2,1)} async-done(((bf16[4,16,4096]{2,1,0:T(8,128)(2,1)}), bf16[32,16,4096]{2,1,0:T(8,128)(2,1)}) %all-gather.8.cloned.1.call-update) | async-done | bytes 4194320 | tf_op jit(solution)/shard_map/all_gather | solution.py:128
  49.4 3.7 pad_maximum_fusion
  57.1 74.7 %all-gather.12.cloned.1.call-done = bf16[4096,512]{1,0:T(8,128)(2,1)} async-done(((bf16[1024,512]{1,0:T(8,128)(2,1)}), bf16[4096,512]{1,0:T(8,128)(2,1)}) %all-gather.12.cloned.1.call-update) | async-done | bytes 4194320 | tf_op jit(solution)/shard_map/all_gather | solution.py:144
  131.8 8.5 %fusion.23 = f32[512,512]{1,0:T(8,128)S(1)} fusion(bf16[4096,512]{1,0:T(8,128)(2,1)} %all-gather.12.cloned.1.call-done, bf16[512,4096]{1,0:T(8,128)(2,1)} %bitcast.105, bf16[512,4096]{1,0:T(8,128)(2,1)} %bitcast.112, f32[4096]{0:T(1024)S(1)} %bitcast.127, bf16[5,32,4096]{2,1,0:T(8,128)(2,1)} %param.27, bf16[512,160]{0,1:T(8,128)(2,1)S(1)} %fusion.28), kind=kOutput, calls=%fused_computation.48 | convolution fusion | flops 2296381440 | bytes 13942784 | tf_op jit(solution)/shard_map/dot_general | solution.py:149
  142.2 70.5 %all-gather.14.cloned.1.call-done = bf16[4096,512]{1,0:T(8,128)(2,1)} async-done(((bf16[1024,512]{1,0:T(8,128)(2,1)}), bf16[4096,512]{1,0:T(8,128)(2,1)}) %all-gather.14.cloned.1.call-update) | async-done | bytes 4194320 | tf_op jit(solution)/shard_map/all_gather | solution.py:143
  212.7 8.6 %fusion.22 = f32[512,512]{1,0:T(8,128)S(1)} fusion(bf16[4096,512]{1,0:T(8,128)(2,1)} %all-gather.14.cloned.1.call-done, bf16[512,4096]{1,0:T(8,128)(2,1)} %bitcast.106, bf16[512,4096]{1,0:T(8,128)(2,1)} %bitcast.113, f32[4096]{0:T(1024)S(1)} %bitcast.126, bf16[5,32,4096]{2,1,0:T(8,128)(2,1)} %param.27, bf16[512,160]{0,1:T(8,128)(2,1)S(1)} %fusion.28), kind=kOutput, calls=%fused_computation.47 | convolution fusion | flops 2296381440 | bytes 13942784 | tf_op jit(solution)/shard_map/dot_general | solution.py:149
  223.1 6.9 %fusion.32 = bf16[512,64]{0,1:T(8,128)(2,1)S(1)} fusion(bf16[4096,64]{0,1:T(8,128)(2,1)S(1)} %copy-done.19, bf16[512,4096]{1,0:T(8,128)(2,1)} %bitcast.107, bf16[512,4096]{1,0:T(8,128)(2,1)} %bitcast.114, f32[4096]{0:T(1024)S(1)} %bitcast.125, bf16[5,32,4096]{2,1,0:T(8,128)(2,1)} %param.27, bf16[512,160]{0,1:T(8,128)(2,1)S(1)} %fusion.28), kind=kOutput, calls=%fused_computation.53 | convolution fusion | flops 417366016 | bytes 9289728 | tf_op jit(solution)/shard_map/dot_general | solution.py:154
  234.1 59.4 %all-gather.10.cloned.1.call-done = bf16[4096,512]{1,0:T(8,128)(2,1)} async-done(((bf16[1024,512]{1,0:T(8,128)(2,1)}), bf16[4096,512]{1,0:T(8,128)(2,1)}) %all-gather.10.cloned.1.call-update) | async-done | bytes 4194320 | tf_op jit(solution)/shard_map/all_gather | solution.py:142
  293.4 8.6 %fusion.24 = f32[512,512]{1,0:T(8,128)S(1)} fusion(bf16[4096,512]{1,0:T(8,128)(2,1)} %all-gather.10.cloned.1.call-done, bf16[512,4096]{1,0:T(8,128)(2,1)} %bitcast.108, bf16[512,4096]{1,0:T(8,128)(2,1)} %bitcast.115, f32[4096]{0:T(1024)S(1)} %bitcast.124, bf16[5,32,4096]{2,1,0:T(8,128)(2,1)} %param.27, bf16[512,160]{0,1:T(8,128)(2,1)} %copy-done.25), kind=kOutput, calls=%fused_computation.49 | convolution fusion | flops 2296381440 | bytes 13942784 | tf_op jit(solution)/shard_map/dot_general | solution.py:149
  305.3 2.2 gather_fusion.5
  307.7 6.3 %exponential_multiply_fusion = (f32[32,16,8,64]{3,2,1,0:T(8,128)}, f32[32,16,8,64]{3,2,1,0:T(8,128)}, f32[32,16,8]{2,1,0:T(8,128)S(1)}, f32[32,16,8,64]{3,2,1,0:T(8,128)}) fusion(f32[32,16,8,64]{3,2,1,0:T(8,128)} %mul.159, f32[32,16,8,64]{3,2,1,0:T(8,128)S(1)} %fusion.77, f32[32,8,64]{2,1,0:T(8,128)S(1)} %get-tuple-element.4, ...), kind=kLoop, calls=%fused_computation.35 | loop fusion | flops 1830912 | bytes 6375936 | tf_op jit(solution)/shard_map/mul | solution.py:81
  314.0 15.2 %multiply_reduce_fusion = f32[32,16,16,8]{3,2,1,0:T(8,128)} fusion(f32[32,16,8,64]{3,2,1,0:T(8,128)S(1)} %fusion.77, f32[32,16,8,64]{3,2,1,0:T(8,128)} %get-tuple-element.10, f32[32,16,8,64]{3,2,1,0:T(8,128)} %mul.159, f32[32,16,8,64]{3,2,1,0:T(8,128)} %reshape.354, pred[16,16]{1,0:T(8,128)(4,1)S(1)} %iota_compare_fusion.3), kind=kLoop, calls=%fused_computation.7 | loop fusion | flops 20905984 | bytes 4456704 | tf_op jit(solution)/shard_map/reduce_sum | solution.py:69
  329.3 4.0 copy.69
  333.3 10.2 %fusion.11 = f32[32,8,16,64]{3,2,1,0:T(8,128)S(1)} fusion(f32[32,8,64,64]{3,2,1,0:T(8,128)} %param.23, f32[32,16,8,64]{3,2,1,0:T(8,128)S(1)} %copy-done.6), kind=kOutput, calls=%fused_computation.33 | convolution fusion | flops 201326592 | bytes 6291456 | tf_op jit(solution)/shard_map/bthi,bhij->bthj/dot_general | solution.py:60
  343.5 3.6 fusion.76
  348.9 4.5 copy.82
  354.2 19.7 %multiply_add_fusion = bf16[32,8,64,64]{3,2,1,0:T(8,128)(2,1)} fusion(f32[32,8,64,64]{3,2,1,0:T(8,128)} %param.23, f32[32,8,64]{2,1,0:T(8,128)S(1)} %get-tuple-element.3, f32[32,16,8,64]{3,2,1,0:T(8,128)} %get-tuple-element.7, f32[32,16,8,64]{3,2,1,0:T(8,128)} %reshape.356), kind=kOutput, calls=%fused_computation.23 | convolution fusion | flops 204472320 | bytes 8454144 | tf_op jit(solution)/shard_map/bshi,bshj->bhij/dot_general | solution.py:82
  373.9 7.8 %gather_fusion = bf16[64,8,64,64]{3,2,1,0:T(8,128)(2,1)} fusion(bf16[32,8,64,64]{3,2,1,0:T(8,128)(2,1)} %multiply_add_fusion, s32[1024]{0:T(1024)S(1)} %pad_clamp_fusion.2), kind=kCustom, calls=%fused_computation | custom fusion | bytes 8388864 | tf_op jit(solution)/shard_map/gather | solution.py:218
  383.2 3.5 all-to-all-start.1
  386.7 10.5 %select_convert_fusion = bf16[4,16,8,64,64]{4,3,2,1,0:T(8,128)(2,1)} fusion(bf16[4,16,8,64,64]{4,3,2,1,0:T(8,128)(2,1)} %bitcast.103, pred[4,16]{1,0:T(4,128)(4,1)S(1)} %and_reduce_fusion), kind=kLoop, calls=%fused_computation.15 | loop fusion | flops 2097152 | bytes 8388672 | tf_op jit(solution)/shard_map/convert_element_type | solution.py:225
  397.3 2.2 copy.72
  403.4 9.7 %reshape.439 = bf16[4,2,262144]{2,1,0:T(2,128)(2,1)} reshape(bf16[4,16,8,64,64]{4,3,2,1,0:T(8,128)(2,1)} %select_convert_fusion) | data formatting | bytes 8388608
  413.1 5.1 all-to-all-start
  418.5 9.7 %multiply_convert_fusion = bf16[512,512]{1,0:T(8,128)(2,1)} fusion(bf16[4096,512]{1,0:T(8,128)(2,1)} %all-gather.16.cloned.1.call-done, bf16[512,4096]{1,0:T(8,128)(2,1)} %bitcast.109, bf16[512,4096]{1,0:T(8,128)(2,1)} %bitcast.116, f32[4096]{0:T(1024)S(1)} %bitcast.123, f32[512,512]{1,0:T(8,128)S(1)} %copy-done.12, f32[512,512]{1,0:T(8,128)S(1)} %copy-done.11, ...), kind=kOutput, calls=%fused_computation.57 | convolution fusion | flops 2299002880 | bytes 16568320 | tf_op jit(solution)/shard_map/dot_general | solution.py:149
  428.2 67.7 %all-gather.18.cloned.1.call-done = bf16[512,4096]{1,0:T(8,128)(2,1)} async-done(((bf16[512,1024]{1,0:T(8,128)(2,1)}), bf16[512,4096]{1,0:T(8,128)(2,1)}) %all-gather.18.cloned.1.call-update) | async-done | bytes 4194320 | tf_op jit(solution)/shard_map/all_gather | solution.py:180
  495.9 6.7 %convolution_convert_fusion = bf16[512,4096]{1,0:T(8,128)(2,1)} fusion(bf16[512,512]{1,0:T(8,128)(2,1)} %multiply_convert_fusion, bf16[512,4096]{1,0:T(8,128)(2,1)} %all-gather.18.cloned.1.call-done), kind=kOutput, calls=%fused_computation.24 | convolution fusion | flops 2149580800 | bytes 8912896 | tf_op jit(solution)/shard_map/dot_general | solution.py:182
  505.6 40.1 %all-to-all-done = bf16[4,2,262144]{2,1,0:T(2,128)(2,1)} async-done(((bf16[4,2,262144]{2,1,0:T(2,128)(2,1)}), bf16[4,2,262144]{2,1,0:T(2,128)(2,1)}, u32[]{:S(2)}, u32[]{:S(2)}) %all-to-all-start) | async-done | bytes 4194336 | tf_op jit(solution)/shard_map/all_to_all | solution.py:224
  545.7 9.3 %reshape.440 = bf16[4,16,8,64,64]{4,3,2,1,0:T(8,128)(2,1)} reshape(bf16[4,2,262144]{2,1,0:T(2,128)(2,1)} %all-to-all-done) | data formatting | bytes 8388608
  555.0 11.3 %bitcast_convert_fusion = f32[64,8,64,64]{3,2,1,0:T(8,128)} fusion(bf16[4,16,8,64,64]{4,3,2,1,0:T(8,128)(2,1)} %reshape.440), kind=kLoop, calls=%fused_computation.22 | loop fusion | flops 2097152 | bytes 12582912 | tf_op jit(solution)/shard_map/reshape | solution.py:236
  566.3 10.4 %gather_fusion.2 = f32[32,8,64,64]{3,2,1,0:T(8,128)} fusion(f32[64,8,64,64]{3,2,1,0:T(8,128)} %bitcast_convert_fusion, s32[1024]{0:T(1024)S(1)} %pad_clamp_fusion), kind=kCustom, calls=%fused_computation.2 | custom fusion | bytes 8388736 | tf_op jit(solution)/shard_map/gather | solution.py:236
  576.7 2.1 fusion.34
  (133 shorter events, 31.8 us)
Async XLA Ops:
  7.2 47.9 %copy-start = (bf16[4096,160]{0,1:T(8,128)(2,1)S(1)}, bf16[4096,160]{0,1:T(8,128)(2,1)}, u32[]{:S(2)}) copy-start(bf16[4096,160]{0,1:T(8,128)(2,1)} %param.26) | copy-start | bytes 3932164
  7.2 4.0 copy-start.18
  7.2 4.2 copy-start.24
  7.2 5.0 copy-start.15
  7.2 16.4 %copy-start.14 = (f32[5,4096]{1,0:T(8,128)S(1)}, f32[5,4096]{1,0:T(8,128)}, u32[]{:S(2)}) copy-start(f32[5,4096]{1,0:T(8,128)} %param.25) | copy-start | bytes 245764
  7.2 42.2 %all-gather.8.cloned.1.call-start = ((), (), s32[]{:S(2)}) async-start(), calls=%async_computation.3 | async-start | bytes 4718592 | tf_op jit(solution)/shard_map/all_gather | solution.py:128
  8.0 123.8 %all-gather.12.cloned.1.call-start = ((), (), s32[]{:S(2)}) async-start(), calls=%async_computation.5 | async-start | bytes 5242880 | tf_op jit(solution)/shard_map/all_gather | solution.py:144
  8.7 204.0 %all-gather.14.cloned.1.call-start = ((), (), s32[]{:S(2)}) async-start(), calls=%async_computation.6 | async-start | bytes 5242880 | tf_op jit(solution)/shard_map/all_gather | solution.py:143
  9.4 284.0 %all-gather.10.cloned.1.call-start = ((), (), s32[]{:S(2)}) async-start(), calls=%async_computation.4 | async-start | bytes 5242880 | tf_op jit(solution)/shard_map/all_gather | solution.py:142
  10.0 408.5 %all-gather.16.cloned.1.call-start = ((), (), s32[]{:S(2)}) async-start(), calls=%async_computation.7 | async-start | bytes 5242880 | tf_op jit(solution)/shard_map/all_gather | solution.py:145
  10.6 485.3 %all-gather.18.cloned.1.call-start = ((), (), s32[]{:S(2)}) async-start(), calls=%async_computation.8 | async-start | bytes 5242880 | tf_op jit(solution)/shard_map/all_gather | solution.py:180
  23.1 30.1 %copy-start.8 = (bf16[32,1,4096]{2,0,1:T(8,128)(2,1)}, bf16[32,1,4096]{2,0,1:T(8,128)(2,1)S(1)}, u32[]{:S(2)}) copy-start(bf16[32,1,4096]{2,0,1:T(8,128)(2,1)S(1)} %broadcast_in_dim.75) | copy-start | bytes 786436
  49.4 5.7 copy-start.3
  49.4 5.7 copy-start.20
  57.1 166.0 %copy-start.25 = (bf16[512,160]{0,1:T(8,128)(2,1)}, bf16[512,160]{0,1:T(8,128)(2,1)S(1)}, u32[]{:S(2)}) copy-start(bf16[512,160]{0,1:T(8,128)(2,1)S(1)} %fusion.28) | copy-start | bytes 491524
  212.7 10.4 %copy-start.19 = (bf16[4096,64]{0,1:T(8,128)(2,1)S(1)}, bf16[4096,64]{0,1:T(8,128)(2,1)}, u32[]{:S(2)}) copy-start(bf16[4096,64]{0,1:T(8,128)(2,1)} %param.29) | copy-start | bytes 1572868
  223.1 6.9 %copy-start.13 = (bf16[64,512]{1,0:T(8,128)(2,1)S(1)}, bf16[64,512]{1,0:T(8,128)(2,1)}, u32[]{:S(2)}) copy-start(bf16[64,512]{1,0:T(8,128)(2,1)} %param.30) | copy-start | bytes 196612
  223.1 6.9 %copy-start.17 = (f32[512]{0:T(512)S(1)}, f32[512]{0:T(512)}, u32[]{:S(2)}) copy-start(f32[512]{0:T(512)} %param.28) | copy-start | bytes 6148
  302.0 5.6 copy-start.16
  329.3 4.0 copy-start.6
  333.3 10.2 %copy-start.2 = (f32[32,16,8,64]{3,2,1,0:T(8,128)S(1)}, f32[32,16,8,64]{3,2,1,0:T(8,128)}, u32[]{:S(2)}) copy-start(f32[32,16,8,64]{3,2,1,0:T(8,128)} %reshape.356) | copy-start | bytes 3145732
  333.3 10.2 %copy-start.5 = (f32[32,16,16,8]{2,1,3,0:T(8,128)S(1)}, f32[32,16,16,8]{2,1,3,0:T(8,128)}, u32[]{:S(2)}) copy-start(f32[32,16,16,8]{2,1,3,0:T(8,128)} %copy.69) | copy-start | bytes 786436
  348.8 4.5 copy-start.9
  383.2 29.9 %all-to-all-start.1 = ((bf16[4,16,512]{2,1,0:T(8,128)(2,1)}), bf16[4,16,512]{2,1,0:T(8,128)(2,1)S(1)}, u32[]{:S(2)}, u32[]{:S(2)}) async-start(bf16[4,16,512]{2,1,0:T(8,128)(2,1)} %fusion.56), calls=%async_computation.2 | async-start | bytes 131072 | tf_op jit(solution)/shard_map/all_to_all | solution.py:227
  413.1 5.4 copy-start.11
  413.1 5.4 copy-start.12
  413.1 5.5 copy-start.21
  413.1 5.5 copy-start.22
  413.1 132.6 %all-to-all-start = ((bf16[4,2,262144]{2,1,0:T(2,128)(2,1)}), bf16[4,2,262144]{2,1,0:T(2,128)(2,1)}, u32[]{:S(2)}, u32[]{:S(2)}) async-start(bf16[4,2,262144]{2,1,0:T(2,128)(2,1)} %reshape.439), calls=%async_computation.1 | async-start | bytes 8388608 | tf_op jit(solution)/shard_map/all_to_all | solution.py:224
  418.2 158.5 %reduce-scatter.2.cloned.1.call-start = ((), (), s32[]{:S(2)}) async-start(), calls=%async_computation.9 | async-start | bytes 4718592 | tf_op jit(solution)/shard_map/reduce_scatter | solution.py:181
  566.3 10.4 %copy-start.10 = (bf16[4,16,4096]{2,1,0:T(8,128)(2,1)S(1)}, bf16[4,16,4096]{2,1,0:T(8,128)(2,1)}, u32[]{:S(2)}) copy-start(bf16[4,16,4096]{2,1,0:T(8,128)(2,1)} %param.21) | copy-start | bytes 1572868
  566.3 12.5 %copy-start.1 = (bf16[4096,160]{0,1:T(8,128)(2,1)S(1)}, bf16[4096,160]{0,1:T(8,128)(2,1)}, u32[]{:S(2)}) copy-start(bf16[4096,160]{0,1:T(8,128)(2,1)} %param.26) | copy-start | bytes 3932164
  (3 other events, 4.5 us)
Sparse Core Ops, SparseCore 0:
  9.9 39.4 all-gather.7
  51.0 80.7 all-gather.11
  133.4 79.2 all-gather.13
  214.1 79.2 all-gather.9
  294.9 79.2 all-gather.15
  375.6 120.2 all-gather.17
  502.8 49.4 reduce-scatter.1
where the time goes:
time: 590 us; the launch traced here: 586 us
  waiting for transfers between devices  342 us (58%)
  matrix products  84.8 us (14%)
  local copies, waits for them, and re-layouts  70.2 us (12%)
  other arithmetic  54.3 us (9%)
  between operations  15 us (3%)
  blocking collectives  10.8 us (2%)
  starting transfers between devices  9.1 us (2%)
    all_gather x1, waiting for transfers between devices, on_device(): lax.all_gather(payload_matrix, 'dp', axis=0, tiled=True)  74.7 us
    all_gather x1, waiting for transfers between devices, on_device(): lax.all_gather(lookup_matrix, 'dp', axis=0, tiled=True)  70.5 us
    all_gather x1, waiting for transfers between devices, on_device(): out_cols = lax.all_gather(emission_matrix, 'dp', axis=1, tiled=True)  67.7 us
    all_gather x1, waiting for transfers between devices, on_device(): lax.all_gather(acceptor_matrix, 'dp', axis=0, tiled=True)  59.4 us
    all_to_all x1, waiting for transfers between devices, on_device(): lax.all_to_all(send_state.astype(jnp.bfloat16), 'dp', split_axis=0, conca...  40.1 us
    dot_general x4, matrix products, on_device(): jnp.dot(source_rows, piece, preferred_element_type=jnp.float32)  35.4 us
    all_gather x1, waiting for transfers between devices, on_device(): lax.all_gather(guess_vectors, 'mp', axis=0, tiled=True)  25.6 us
    unnamed x55, local copies, waits for them, and re-layouts  21.5 us
  transfers between devices with their start and end apart: 9, of which 6 were waited for; matrix products, arithmetic and copies ran while one was open for 35% of the time, Pallas kernels for 0%

commit v1 on v0

--- a/solution.py
+++ b/solution.py
@@ -5,6 +5,29 @@
 
 GROUP_DIMENSION = 64
 norm_eps = 0.00064
+
+
+def laid_out(pieces, dim):
+    lengths = list(pieces.shape[1:])
+    lengths[dim] *= pieces.shape[0]
+    return jnp.moveaxis(pieces, 0, dim).reshape(lengths)
+
+
+def doubled(array, axis):
+    size, place = (lax.axis_size(axis), lax.axis_index(axis))
+    blocks, apart = (array[None], 1)
+    while apart < size:
+        received = lax.ppermute(blocks, axis, [(i, i ^ apart) for i in range(size)])
+        low = place & apart == 0
+        blocks = jnp.concatenate(
+            [jnp.where(low, blocks, received), jnp.where(low, received, blocks)]
+        )
+        apart *= 2
+    return blocks
+
+
+def collect(x, axis, dim):
+    return laid_out(doubled(x, axis), dim)
 
 
 def token_mixes(
@@ -139,7 +162,7 @@
     token_rows = row_reqs * draft
     sources = (shift_mixed_rows[3], shift_mixed_rows[1], shift_mixed_rows[2], shift_mixed_rows[4])
     pieces = (
-        lax.all_gather(acceptor_matrix, "dp", axis=0, tiled=True),
+        collect(acceptor_matrix, "dp", 0),
         lax.all_gather(lookup_matrix, "dp", axis=0, tiled=True),
         lax.all_gather(payload_matrix, "dp", axis=0, tiled=True),
         lax.all_gather(gating_matrix, "dp", axis=0, tiled=True),

time: 590 us -> 572 us (0.969)
  waiting for transfers between devices: 342 us -> 276 us
  other arithmetic: 54.3 us -> 74.7 us
  local copies, waits for them, and re-layouts: 70.2 us -> 84.7 us
    ppermute x0 -> x2, waiting for transfers between devices: none -> 170 us  [doubled(): received = lax.ppermute(blocks, axis, [(i, i ^ apart) for i in range(size)])]
    all_gather x1, waiting for transfers between devices: 70.5 us -> 0.01 us  [on_device(): lax.all_gather(lookup_matrix, 'dp', axis=0, tiled=True)]
    all_gather x1, waiting for transfers between devices: 74.7 us -> 8.35 us  [on_device(): lax.all_gather(payload_matrix, 'dp', axis=0, tiled=True)]
    all_gather x1 -> x0, waiting for transfers between devices: 59.4 us -> none  [on_device(): lax.all_gather(acceptor_matrix, 'dp', axis=0, tiled=True)]
    all_gather x1, waiting for transfers between devices: 25.6 us -> 0.01 us  [on_device(): lax.all_gather(guess_vectors, 'mp', axis=0, tiled=True)]
    all_gather x1, waiting for transfers between devices: 67.7 us -> 49.4 us  [on_device(): out_cols = lax.all_gather(emission_matrix, 'dp', axis=1, tiled=True)]
    another operation x1, other arithmetic: 1.75 us -> 19.5 us  [wkv_blocks(): cumulative = jnp.cumsum(logarithmic_fading_entries, axis=1)]
    dot_general x0 -> x1, matrix products: none -> 7.67 us  [token_mixes(): jnp.dot(mixing_inner_all[:, mix_component * mixing_inner_width:(mix_compo...]
  transfers between devices with their start and end apart: 9 -> 10, of which waited for: 6 -> 5; matrix products, arithmetic and copies ran while one was open for 35% -> 43% of each run, Pallas kernels for 0% -> 0%
where the time goes in v1:
time: 572 us; the launch traced here: 564 us
  waiting for transfers between devices  276 us (48%)
  matrix products  88.8 us (16%)
  local copies, waits for them, and re-layouts  84.7 us (15%)
  other arithmetic  74.7 us (13%)
  between operations  15.3 us (3%)
  starting transfers between devices  14.9 us (3%)
  blocking collectives  9.32 us (2%)
    ppermute x2, waiting for transfers between devices, doubled(): received = lax.ppermute(blocks, axis, [(i, i ^ apart) for i in range(size)])  170 us
    all_gather x1, waiting for transfers between devices, on_device(): out_cols = lax.all_gather(emission_matrix, 'dp', axis=1, tiled=True)  49.4 us
    all_to_all x1, waiting for transfers between devices, on_device(): lax.all_to_all(send_state.astype(jnp.bfloat16), 'dp', split_axis=0, conca...  46.1 us
    dot_general x4, matrix products, on_device(): jnp.dot(source_rows, piece, preferred_element_type=jnp.float32)  33.6 us
    unnamed x76, local copies, waits for them, and re-layouts  24.5 us
    another operation x1, other arithmetic, wkv_blocks(): cumulative = jnp.cumsum(logarithmic_fading_entries, axis=1)  19.5 us
    dot_general x1, matrix products, wkv_blocks(): jnp.einsum('bshi,bshj->bhij', weighted, payload_vectors, precision=lax.Pr...  18.1 us
    reduce_sum x1, other arithmetic, wkv_blocks(): jnp.sum(acceptor_vectors[:, :, None] * lookup_vectors[:, None, :] * jnp.e...  14.9 us
  transfers between devices with their start and end apart: 10, of which 5 were waited for; matrix products, arithmetic and copies ran while one was open for 43% of the time, Pallas kernels for 0%

profile of v1, /device:TPU:0, one launch (start us, length us, event | category | flops | bytes accessed | tf_op | source)
XLA Modules:
  0.0 563.7 jit_solution(9663780871716190945)
XLA Ops:
  13.4 9.3 %all-gather = bf16[8,4,4096]{2,1,0:T(4,128)(2,1)S(1)} all-gather(bf16[1,4,4096]{2,1,0:T(4,128)(2,1)S(1)} %bitcast.139), channel_id=1, replica_groups=mesh['dp'=4,'mp'=8] {'mp'}, dimensions={0}, use_global_device_ids=true | all-gather | bytes 294912 | tf_op jit(solution)/shard_map/all_gather | solution.py:152
  23.9 12.7 %collective-permute-done = bf16[1,1024,512]{2,1,0:T(8,128)(2,1)} collective-permute-done((bf16[1,1024,512]{2,1,0:T(8,128)(2,1)}, bf16[1,1024,512]{2,1,0:T(8,128)(2,1)}, u32[]{:S(2)}, u32[]{:S(2)}) %collective-permute-start) | collective-permute-done | bytes 1048608 | tf_op jit(solution)/shard_map/ppermute | solution.py:20
  41.5 156.9 %collective-permute-done.1 = bf16[2,1024,512]{2,1,0:T(8,128)(2,1)S(1)} collective-permute-done((bf16[2,1024,512]{2,1,0:T(8,128)(2,1)S(1)}, bf16[2,1024,512]{2,1,0:T(8,128)(2,1)S(1)}, u32[]{:S(2)}, u32[]{:S(2)}) %collective-permute-start.1) | collective-permute-done | bytes 2097184 | tf_op jit(solution)/shard_map/ppermute | solution.py:20
  201.0 6.4 %copy.88 = bf16[4096,512]{0,1:T(8,128)(2,1)} copy(bf16[4096,512]{1,0:T(8,128)(2,1)} %bitcast.125) | data formatting | bytes 8388608 | tf_op jit(solution)/shard_map/reshape | solution.py:13
  207.4 3.5 pad_maximum_fusion
  213.0 7.0 %fusion.33 = bf16[512,64]{0,1:T(8,128)(2,1)S(1)} fusion(bf16[4096,64]{0,1:T(8,128)(2,1)S(1)} %copy-done.28, bf16[512,4096]{1,0:T(8,128)(2,1)} %bitcast.119, bf16[512,4096]{1,0:T(8,128)(2,1)} %bitcast.127, f32[4096]{0:T(1024)S(1)} %bitcast.144, bf16[5,32,4096]{2,1,0:T(8,128)(2,1)} %param.27, bf16[512,160]{0,1:T(8,128)(2,1)S(1)} %fusion.29), kind=kOutput, calls=%fused_computation.57 | convolution fusion | flops 417366016 | bytes 9289728 | tf_op jit(solution)/shard_map/dot_general | solution.py:177
  220.8 19.5 %fusion.77 = f32[32,16,8,64]{3,2,1,0:T(8,128)S(1)} fusion(f32[32,16,8,64]{3,2,1,0:T(8,128)S(1)} %reshape.358), kind=kOutput, calls=%fused_computation.133 | output fusion | flops 3932160 | bytes 2097152 | tf_op jit(solution)/shard_map/jit(cumsum)/reduce_window_sum | solution.py:78
  244.5 8.6 %fusion.24 = f32[512,512]{1,0:T(8,128)S(1)} fusion(bf16[4096,512]{1,0:T(8,128)(2,1)} %all-gather.11.cloned.1.call-done, bf16[512,4096]{1,0:T(8,128)(2,1)} %bitcast.120, bf16[512,4096]{1,0:T(8,128)(2,1)} %bitcast.128, f32[4096]{0:T(1024)S(1)} %bitcast.143, bf16[5,32,4096]{2,1,0:T(8,128)(2,1)} %param.27, bf16[512,160]{0,1:T(8,128)(2,1)S(1)} %copy-done.35), kind=kOutput, calls=%fused_computation.52 | convolution fusion | flops 2296381440 | bytes 13942784 | tf_op jit(solution)/shard_map/dot_general | solution.py:172
  254.9 7.7 %fusion.1 = bf16[512,4096]{1,0:T(8,128)(2,1)} fusion(bf16[512,4096]{1,0:T(8,128)(2,1)} %bitcast.121, bf16[512,4096]{1,0:T(8,128)(2,1)} %bitcast.129, f32[4096]{0:T(1024)S(1)} %bitcast.142, bf16[5,32,4096]{2,1,0:T(8,128)(2,1)} %param.27, bf16[512,160]{0,1:T(8,128)(2,1)S(1)} %copy-done.35), kind=kOutput, calls=%fused_computation.17 | convolution fusion | flops 148897792 | bytes 12894208 | tf_op jit(solution)/shard_map/dot_general | solution.py:52
  262.6 8.3 %all-gather.9.cloned.1.call-done = bf16[4096,512]{1,0:T(8,128)(2,1)} async-done(((bf16[1024,512]{1,0:T(8,128)(2,1)}), bf16[4096,512]{1,0:T(8,128)(2,1)}) %all-gather.9.cloned.1.call-update) | async-done | bytes 4194320 | tf_op jit(solution)/shard_map/all_gather | solution.py:167
  270.9 8.6 %fusion.25 = f32[512,512]{1,0:T(8,128)S(1)} fusion(bf16[4096,512]{1,0:T(8,128)(2,1)} %all-gather.9.cloned.1.call-done, bf16[512,4096]{1,0:T(8,128)(2,1)} %bitcast.122, bf16[512,4096]{1,0:T(8,128)(2,1)} %bitcast.130, f32[4096]{0:T(1024)S(1)} %bitcast.141, bf16[5,32,4096]{2,1,0:T(8,128)(2,1)} %param.27, bf16[512,160]{0,1:T(8,128)(2,1)S(1)} %copy-done.35), kind=kOutput, calls=%fused_computation.53 | convolution fusion | flops 2296381440 | bytes 13942784 | tf_op jit(solution)/shard_map/dot_general | solution.py:172
  281.3 4.0 copy.91
  285.3 6.7 %fusion.78 = f32[32,16,8,64]{3,1,2,0:T(8,128)S(1)} fusion(bf16[32,16,4096,1]{2,1,3,0:T(8,128)(2,1)} %bitcast.145, bf16[8,64,4096,1]{2,1,0,3:T(8,128)(2,1)S(1)} %bitcast.132), kind=kOutput, calls=%fused_computation.134 | convolution fusion | flops 2147483648 | bytes 9437184 | tf_op jit(solution)/shard_map/dot_general | solution.py:172
  296.4 14.9 %multiply_reduce_fusion = f32[32,16,16,8]{3,2,1,0:T(8,128)} fusion(f32[32,16,8,64]{3,2,1,0:T(8,128)S(1)} %copy-done.3, f32[32,16,8,64]{3,2,1,0:T(8,128)} %copy.91, f32[32,16,8,64]{3,2,1,0:T(8,128)S(1)} %copy-done.5, f32[32,16,8,64]{3,2,1,0:T(8,128)} %copy.90, pred[16,16]{1,0:T(8,128)(4,1)S(1)} %iota_compare_fusion.3), kind=kLoop, calls=%fused_computation.7 | loop fusion | flops 20905984 | bytes 4456704 | tf_op jit(solution)/shard_map/reduce_sum | solution.py:92
  311.3 3.8 copy.93
  318.1 10.1 %fusion.12 = f32[32,8,16,64]{3,2,1,0:T(8,128)S(1)} fusion(f32[32,8,64,64]{3,2,1,0:T(8,128)} %param.23, f32[32,16,8,64]{3,1,2,0:T(8,128)S(1)} %copy-done.7, f32[32,16,8,64]{3,1,2,0:T(8,128)S(1)} %copy.89), kind=kOutput, calls=%fused_computation.39 | convolution fusion | flops 201588736 | bytes 7340032 | tf_op jit(solution)/shard_map/bthi,bhij->bthj/dot_general | solution.py:83
  328.3 3.3 fusion.76
  333.3 3.1 concatenate.18.clone
  338.7 4.5 copy.107
  346.8 18.1 %multiply_add_fusion = bf16[32,8,64,64]{3,2,1,0:T(8,128)(2,1)} fusion(f32[32,8,64,64]{3,2,1,0:T(8,128)} %param.23, f32[32,8,64]{2,1,0:T(8,128)S(1)} %get-tuple-element.3, f32[32,16,8,64]{3,2,1,0:T(8,128)S(1)} %exponential_multiply_fusion, f32[32,16,8,64]{3,2,1,0:T(8,128)S(1)} %copy-done.11), kind=kOutput, calls=%fused_computation.23 | convolution fusion | flops 204472320 | bytes 8454144 | tf_op jit(solution)/shard_map/bshi,bshj->bhij/dot_general | solution.py:105
  364.9 8.0 %gather_fusion = bf16[64,8,64,64]{3,2,1,0:T(8,128)(2,1)} fusion(bf16[32,8,64,64]{3,2,1,0:T(8,128)(2,1)} %multiply_add_fusion, s32[1024]{0:T(1024)S(1)} %pad_clamp_fusion.2), kind=kCustom, calls=%fused_computation | custom fusion | bytes 8388864 | tf_op jit(solution)/shard_map/gather | solution.py:241
  374.4 3.3 all-to-all-start.1
  377.7 10.7 %select_convert_fusion = bf16[4,16,8,64,64]{4,3,2,1,0:T(8,128)(2,1)} fusion(bf16[4,16,8,64,64]{4,3,2,1,0:T(8,128)(2,1)} %bitcast.117, pred[4,16]{1,0:T(4,128)(4,1)S(1)} %and_reduce_fusion), kind=kLoop, calls=%fused_computation.15 | loop fusion | flops 2097152 | bytes 8388672 | tf_op jit(solution)/shard_map/convert_element_type | solution.py:248
  393.2 9.6 %reshape.444 = bf16[4,2,262144]{2,1,0:T(2,128)(2,1)} reshape(bf16[4,16,8,64,64]{4,3,2,1,0:T(8,128)(2,1)} %select_convert_fusion) | data formatting | bytes 8388608
  402.9 5.2 all-to-all-start
  408.4 9.7 %multiply_convert_fusion = bf16[512,512]{1,0:T(8,128)(2,1)} fusion(bf16[4096,512]{1,0:T(8,128)(2,1)} %all-gather.13.cloned.1.call-done, bf16[512,4096]{1,0:T(8,128)(2,1)} %bitcast.123, bf16[512,4096]{1,0:T(8,128)(2,1)} %bitcast.131, f32[4096]{0:T(1024)S(1)} %bitcast.140, f32[512,512]{1,0:T(8,128)S(1)} %copy-done.21, f32[512,512]{1,0:T(8,128)S(1)} %copy-done.20, ...), kind=kOutput, calls=%fused_computation.61 | convolution fusion | flops 2299002880 | bytes 16568320 | tf_op jit(solution)/shard_map/dot_general | solution.py:172
  418.1 49.4 %all-gather.15.cloned.1.call-done = bf16[512,4096]{1,0:T(8,128)(2,1)} async-done(((bf16[512,1024]{1,0:T(8,128)(2,1)}), bf16[512,4096]{1,0:T(8,128)(2,1)}) %all-gather.15.cloned.1.call-update) | async-done | bytes 4194320 | tf_op jit(solution)/shard_map/all_gather | solution.py:203
  467.5 6.7 %convolution_convert_fusion = bf16[512,4096]{1,0:T(8,128)(2,1)} fusion(bf16[512,512]{1,0:T(8,128)(2,1)} %multiply_convert_fusion, bf16[512,4096]{1,0:T(8,128)(2,1)} %all-gather.15.cloned.1.call-done), kind=kOutput, calls=%fused_computation.24 | convolution fusion | flops 2149580800 | bytes 8912896 | tf_op jit(solution)/shard_map/dot_general | solution.py:205
  477.2 46.1 %all-to-all-done = bf16[4,2,262144]{2,1,0:T(2,128)(2,1)} async-done(((bf16[4,2,262144]{2,1,0:T(2,128)(2,1)}), bf16[4,2,262144]{2,1,0:T(2,128)(2,1)}, u32[]{:S(2)}, u32[]{:S(2)}) %all-to-all-start) | async-done | bytes 4194336 | tf_op jit(solution)/shard_map/all_to_all | solution.py:247
  523.3 9.3 %reshape.445 = bf16[4,16,8,64,64]{4,3,2,1,0:T(8,128)(2,1)} reshape(bf16[4,2,262144]{2,1,0:T(2,128)(2,1)} %all-to-all-done) | data formatting | bytes 8388608
  532.6 11.4 %bitcast_convert_fusion = f32[64,8,64,64]{3,2,1,0:T(8,128)} fusion(bf16[4,16,8,64,64]{4,3,2,1,0:T(8,128)(2,1)} %reshape.445), kind=kLoop, calls=%fused_computation.22 | loop fusion | flops 2097152 | bytes 12582912 | tf_op jit(solution)/shard_map/reshape | solution.py:259
  544.0 10.4 %gather_fusion.2 = f32[32,8,64,64]{3,2,1,0:T(8,128)} fusion(f32[64,8,64,64]{3,2,1,0:T(8,128)} %bitcast_convert_fusion, s32[1024]{0:T(1024)S(1)} %pad_clamp_fusion), kind=kCustom, calls=%fused_computation.2 | custom fusion | bytes 8388736 | tf_op jit(solution)/shard_map/gather | solution.py:259
  (164 shorter events, 51.6 us)
Async XLA Ops:
  7.2 203.7 %copy-start = (bf16[4096,160]{0,1:T(8,128)(2,1)S(1)}, bf16[4096,160]{0,1:T(8,128)(2,1)}, u32[]{:S(2)}) copy-start(bf16[4096,160]{0,1:T(8,128)(2,1)} %param.26) | copy-start | bytes 3932164
  7.2 29.4 %copy-start.19 = (bf16[1024,512]{1,0:T(8,128)(2,1)S(1)}, bf16[1024,512]{1,0:T(8,128)(2,1)}, u32[]{:S(2)}) copy-start(bf16[1024,512]{1,0:T(8,128)(2,1)} %param.32) | copy-start | bytes 3145732
  7.2 6.0 %copy-start.33 = (s32[128]{0:T(128)S(1)}, s32[128]{0:T(128)}, u32[]{:S(2)}) copy-start(s32[128]{0:T(128)} %param.41) | copy-start | bytes 1540
  7.2 6.2 %copy-start.24 = (bf16[4,4096]{1,0:T(4,128)(2,1)S(1)}, bf16[4,4096]{1,0:T(4,128)(2,1)}, u32[]{:S(2)}) copy-start(bf16[4,4096]{1,0:T(4,128)(2,1)} %param.22) | copy-start | bytes 98308
  7.2 200.2 %all-gather.7.cloned.1.call-start = ((), (), s32[]{:S(2)}) async-start(), calls=%async_computation.3 | async-start | bytes 4718592 | tf_op jit(solution)/shard_map/all_gather | solution.py:151
  7.9 236.6 %all-gather.11.cloned.1.call-start = ((), (), s32[]{:S(2)}) async-start(), calls=%async_computation.5 | async-start | bytes 5242880 | tf_op jit(solution)/shard_map/all_gather | solution.py:166
  8.7 262.2 %all-gather.9.cloned.1.call-start = ((), (), s32[]{:S(2)}) async-start(), calls=%async_computation.4 | async-start | bytes 5242880 | tf_op jit(solution)/shard_map/all_gather | solution.py:167
  9.4 399.0 %all-gather.13.cloned.1.call-start = ((), (), s32[]{:S(2)}) async-start(), calls=%async_computation.6 | async-start | bytes 5242880 | tf_op jit(solution)/shard_map/all_gather | solution.py:168
  10.0 457.5 %all-gather.15.cloned.1.call-start = ((), (), s32[]{:S(2)}) async-start(), calls=%async_computation.7 | async-start | bytes 5242880 | tf_op jit(solution)/shard_map/all_gather | solution.py:203
  10.1 26.6 %collective-permute-start = (bf16[1,1024,512]{2,1,0:T(8,128)(2,1)}, bf16[1,1024,512]{2,1,0:T(8,128)(2,1)}, u32[]{:S(2)}, u32[]{:S(2)}) collective-permute-start(bf16[1,1024,512]{2,1,0:T(8,128)(2,1)} %bitcast.136), channel_id=1, source_target_pairs={{0,8},{8,0},{16,24},{24,16},{1,9},{9,1},{17,25},{25,17},{2,10},{10... | collective-permute-start | bytes 3145736 | tf_op jit(solution)/shard_map/ppermute | solution.py:20
  22.8 15.4 %copy-start.16 = (bf16[32,1,4096]{2,0,1:T(8,128)(2,1)}, bf16[32,1,4096]{2,0,1:T(8,128)(2,1)S(1)}, u32[]{:S(2)}) copy-start(bf16[32,1,4096]{2,0,1:T(8,128)(2,1)S(1)} %broadcast_in_dim.77) | copy-start | bytes 786436
  23.9 17.1 %copy-start.27 = (s32[128]{0:T(128)S(1)}, s32[128]{0:T(128)}, u32[]{:S(2)}) copy-start(s32[128]{0:T(128)} %param.40) | copy-start | bytes 1540
  23.9 17.5 %copy-start.23 = (f32[5,4096]{1,0:T(8,128)S(1)}, f32[5,4096]{1,0:T(8,128)}, u32[]{:S(2)}) copy-start(f32[5,4096]{1,0:T(8,128)} %param.25) | copy-start | bytes 245764
  38.2 160.2 %collective-permute-start.1 = (bf16[2,1024,512]{2,1,0:T(8,128)(2,1)S(1)}, bf16[2,1024,512]{2,1,0:T(8,128)(2,1)S(1)}, u32[]{:S(2)}, u32[]{:S(2)}) collective-permute-start(bf16[2,1024,512]{2,1,0:T(8,128)(2,1)S(1)} %pad_maximum_fusion.2), channel_id=1, source_target_pairs={{0,16},{8,24},{16,0},{24,8},{1,17},{9,25},{17,1},{25,9},{2,18},{10... | collective-permute-start | bytes 6291464 | tf_op jit(solution)/shard_map/ppermute | solution.py:20
  212.9 7.0 %copy-start.34 = (bf16[512,160]{0,1:T(8,128)(2,1)}, bf16[512,160]{0,1:T(8,128)(2,1)S(1)}, u32[]{:S(2)}) copy-start(bf16[512,160]{0,1:T(8,128)(2,1)S(1)} %fusion.29) | copy-start | bytes 491524
  213.0 7.0 %copy-start.22 = (bf16[64,512]{1,0:T(8,128)(2,1)S(1)}, bf16[64,512]{1,0:T(8,128)(2,1)}, u32[]{:S(2)}) copy-start(bf16[64,512]{1,0:T(8,128)(2,1)} %param.30) | copy-start | bytes 196612
  213.0 7.0 %copy-start.26 = (f32[512]{0:T(512)S(1)}, f32[512]{0:T(512)}, u32[]{:S(2)}) copy-start(f32[512]{0:T(512)} %param.28) | copy-start | bytes 6148
  281.3 4.0 copy-start.15
  318.1 10.2 %copy-start.10 = (f32[32,16,8,64]{3,2,1,0:T(8,128)S(1)}, f32[32,16,8,64]{3,2,1,0:T(8,128)}, u32[]{:S(2)}) copy-start(f32[32,16,8,64]{3,2,1,0:T(8,128)} %reshape.359) | copy-start | bytes 3145732
  318.1 10.2 %copy-start.13 = (f32[32,16,16,8]{2,1,3,0:T(8,128)S(1)}, f32[32,16,16,8]{2,1,3,0:T(8,128)}, u32[]{:S(2)}) copy-start(f32[32,16,16,8]{2,1,3,0:T(8,128)} %copy.93) | copy-start | bytes 786436
  331.6 7.1 %copy-start.8 = (f32[32,16,8,64]{3,1,2,0:T(8,128)}, f32[32,16,8,64]{3,1,2,0:T(8,128)S(1)}, u32[]{:S(2)}) copy-start(f32[32,16,8,64]{3,1,2,0:T(8,128)S(1)} %get-tuple-element.17) | copy-start | bytes 3145732
  338.7 4.5 copy-start.17
  374.4 28.5 %all-to-all-start.1 = ((bf16[4,16,512]{2,1,0:T(8,128)(2,1)}), bf16[4,16,512]{2,1,0:T(8,128)(2,1)S(1)}, u32[]{:S(2)}, u32[]{:S(2)}) async-start(bf16[4,16,512]{2,1,0:T(8,128)(2,1)} %fusion.56), calls=%async_computation.2 | async-start | bytes 131072 | tf_op jit(solution)/shard_map/all_to_all | solution.py:250
  377.7 10.8 %copy-start.9 = (f32[32,16,8,64]{3,1,2,0:T(8,128)S(1)}, f32[32,16,8,64]{3,1,2,0:T(8,128)}, u32[]{:S(2)}) copy-start(f32[32,16,8,64]{3,1,2,0:T(8,128)} %copy-done.8) | copy-start | bytes 3145732
  402.9 5.5 copy-start.20
  402.9 5.5 copy-start.21
  402.9 5.6 copy-start.30
  402.9 5.6 copy-start.31
  402.9 120.4 %all-to-all-start = ((bf16[4,2,262144]{2,1,0:T(2,128)(2,1)}), bf16[4,2,262144]{2,1,0:T(2,128)(2,1)}, u32[]{:S(2)}, u32[]{:S(2)}) async-start(bf16[4,2,262144]{2,1,0:T(2,128)(2,1)} %reshape.444), calls=%async_computation.1 | async-start | bytes 8388608 | tf_op jit(solution)/shard_map/all_to_all | solution.py:247
  408.1 146.2 %reduce-scatter.2.cloned.1.call-start = ((), (), s32[]{:S(2)}) async-start(), calls=%async_computation.8 | async-start | bytes 4718592 | tf_op jit(solution)/shard_map/reduce_scatter | solution.py:204
  544.0 10.4 %copy-start.18 = (bf16[4,16,4096]{2,1,0:T(8,128)(2,1)S(1)}, bf16[4,16,4096]{2,1,0:T(8,128)(2,1)}, u32[]{:S(2)}) copy-start(bf16[4,16,4096]{2,1,0:T(8,128)(2,1)} %param.21) | copy-start | bytes 1572868
  544.0 12.5 %copy-start.1 = (bf16[4096,160]{0,1:T(8,128)(2,1)S(1)}, bf16[4096,160]{0,1:T(8,128)(2,1)}, u32[]{:S(2)}) copy-start(bf16[4096,160]{0,1:T(8,128)(2,1)} %param.26) | copy-start | bytes 3932164
  (14 other events, 35.4 us)
Sparse Core Ops, SparseCore 0:
  9.9 39.4 all-gather.6
  51.0 137.5 all-gather.10
  190.1 80.8 all-gather.8
  272.3 79.2 all-gather.12
  353.1 114.3 all-gather.14
  474.4 49.4 reduce-scatter.1
